TPU v7x, 32 devices: a whole 2x2x4 slice. The times are simulated.
32 devices in a mesh: gx: 8 (over z, x), gy: 4 (over y, core).
Axes of the slice: x: 2, y: 2, z: 4, core: 2. Of those that a mesh axis runs over, the one named last changes fastest.
Arguments:
- hydro: float32 [192, 192, 792], P('gx', 'gy'), may hold values from 0.05 to 2
- winds: float32 [192, 192, 24], P('gx', 'gy'), may hold values from -0.3 to 0.3
- cloud_mask: int32 [192, 192], P('gx', 'gy'), may hold values from 0 to 1, as said below
- coal_kernel: bfloat16 [4356, 66], replicated, may hold values from -0.09375 to 0.09375
- block_mask: int32 [6, 6], replicated, may hold values 0 or 1
Outputs:
- hydro_next: float32 [192, 192, 792], P('gx', 'gy')
Inputs may be any that keep to these rules, and one draw needn't show every extreme that they name: `cloud_mask`: exactly 4608 columns are cloudy; the columns of one aligned tile of 24 x 48 are all cloudy.
All inputs are finite; a program needn't handle non-finite values.
Results may differ from a plain program's by a relative error of at most 0.0017.
Values may be sent and summed in bfloat16 or wider, within the bound.
A program may use at most 128 MiB of HBM per device.

v0:
```python
import jax
import jax.numpy as jnp
from jax import lax
from jax.sharding import PartitionSpec as P

BLK = 11


def padded_2(array, sides, width):
    for axis, dim in sides:
        count, length = (lax.axis_size(axis), array.shape[dim])
        up = [(i, (i + 1) % count) for i in range(count)]
        down = [(j, i) for i, j in up]
        last = lax.slice_in_dim(array, length - width, length, axis=dim)
        initial = lax.slice_in_dim(array, 0, width, axis=dim)
        before = lax.ppermute(last, axis, up)
        after = lax.ppermute(initial, axis, down)
        array = jnp.concatenate([before, array, after], axis=dim)
    return array


def coalesce(rows2d, chan, kernel_wide):
    total = rows2d.shape[0] * (rows2d.shape[1] // chan)
    cells = rows2d.reshape(total, chan)
    pieces = 1
    while total % pieces != 0 or total // pieces > 2048:
        pieces = pieces + 1

    def one_block(block):
        wide = block.astype(jnp.float32)
        pairs = (wide[:, :, None] * wide[:, None, :]).astype(jnp.bfloat16).reshape(-1, chan * chan)
        return jnp.dot(pairs, kernel_wide, preferred_element_type=jnp.float32).astype(jnp.bfloat16)

    result = lax.map(one_block, cells.reshape(pieces, total // pieces, chan))
    result = result.reshape(total, kernel_wide.shape[1])[:, :chan]
    return result.reshape(rows2d.shape[0], rows2d.shape[1])


def per_device(hydro, winds, cloud_mask, coal_kernel, block_mask):
    size_x, size_y, width = hydro.shape
    levels = winds.shape[2] // 2
    chan = width // levels
    stacked = jnp.concatenate([hydro, winds], axis=2)
    padded = padded_2(stacked, (("gx", 0), ("gy", 1)), 1)
    field = padded[:, :, :width]
    wind_x = padded[:, :, width : width + levels]
    wind_y = padded[:, :, width + levels :]
    along_x = field[:, 1:-1]
    face_x = jnp.repeat(0.5 * (wind_x[:-1, 1:-1] + wind_x[1:, 1:-1]), chan, axis=2)
    flux_x = jnp.maximum(face_x, 0.0) * along_x[:-1] + jnp.minimum(face_x, 0.0) * along_x[1:]
    along_y = field[1:-1]
    face_y = jnp.repeat(0.5 * (wind_y[1:-1, :-1] + wind_y[1:-1, 1:]), chan, axis=2)
    flux_y = jnp.maximum(face_y, 0.0) * along_y[:, :-1] + jnp.minimum(face_y, 0.0) * along_y[:, 1:]
    q_adv = field[1:-1, 1:-1] - (flux_x[1:] - flux_x[:-1]) - (flux_y[:, 1:] - flux_y[:, :-1])
    blocks_count = block_mask.shape[0]
    onehot = ((jnp.arange(chan) // BLK)[:, None] == jnp.arange(blocks_count)[None, :]).astype(
        jnp.float32
    )
    blockmap = jnp.dot(jnp.dot(onehot, block_mask.astype(jnp.float32)), onehot.T)
    kernel_eff = jnp.where(
        blockmap.reshape(chan * chan, 1) > 0.5, coal_kernel, jnp.zeros_like(coal_kernel)
    )
    lanes = (chan + 127) // 128 * 128
    kernel_wide = jnp.concatenate(
        [kernel_eff, jnp.zeros((chan * chan, lanes - chan), jnp.bfloat16)], axis=1
    )
    ncols = size_x * size_y
    flat = cloud_mask.reshape(-1)
    columns = q_adv.astype(jnp.bfloat16).reshape(ncols, width)
    size_gx = lax.axis_size("gx")
    size_gy = lax.axis_size("gy")
    devices = size_gx * size_gy
    me_index = lax.axis_index("gx") * size_gy + lax.axis_index("gy")
    count = jnp.sum(flat)
    counts = lax.all_gather(count.reshape(1), ("gx", "gy"), axis=0, tiled=True)
    starts = jnp.cumsum(counts) - counts
    ends = starts + counts
    offset = starts[me_index]
    send_rows = ncols // devices
    owned = ncols // 8
    source_index = jnp.nonzero(flat, size=ncols, fill_value=0)[0].astype(jnp.int32)
    slot_pos = jnp.arange(send_rows, dtype=jnp.int32)[:, None]
    slot_dev = jnp.arange(devices, dtype=jnp.int32)[None, :]
    send_rank = (slot_pos * devices + (slot_dev - offset) % devices).reshape(-1)
    send_alive = send_rank < count
    outgoing = jnp.where(
        send_alive[:, None], columns[source_index[send_rank]], jnp.zeros((), jnp.bfloat16)
    )
    outgoing = outgoing.reshape(send_rows, devices, width)
    position = jnp.arange(send_rows)[:, None]
    rel_rank = position * devices + ((me_index - starts) % devices)[None, :]
    alive_slot = rel_rank < counts[None, :]
    slot_of = jnp.where(alive_slot, (starts[None, :] + rel_rank) // devices, owned)
    global_rank = jnp.arange(owned) * devices + me_index
    source_dev = jnp.sum((ends[None, :] <= global_rank[:, None]).astype(jnp.int32), axis=1)
    local_rank = global_rank - starts[source_dev]
    arrive_row = local_rank // devices * devices + source_dev
    arrived = lax.all_to_all(outgoing, ("gx", "gy"), split_axis=1, concat_axis=1, tiled=True)
    gathered = arrived.reshape(send_rows * devices, width)[arrive_row]
    computed = coalesce(gathered, chan, kernel_wide)
    extended = jnp.concatenate([computed, jnp.zeros((1, width), jnp.bfloat16)], axis=0)
    returned = lax.all_to_all(
        extended[slot_of.reshape(-1)].reshape(send_rows, devices, width),
        ("gx", "gy"),
        split_axis=1,
        concat_axis=1,
        tiled=True,
    )
    returned = returned.reshape(send_rows * devices, width)
    column_rank = jnp.maximum(jnp.cumsum(flat) - 1, 0)
    back_row = column_rank // devices * devices + (column_rank % devices + offset) % devices
    tendency = jnp.where(flat[:, None] > 0, returned[back_row].astype(jnp.float32), 0.0)
    result = q_adv + tendency.reshape(size_x, size_y, width)
    return result


def solution(mesh):
    in_specs = (P("gx", "gy", None), P("gx", "gy", None), P("gx", "gy"), P(), P())
    out_specs = P("gx", "gy", None)
    return jax.shard_map(
        per_device, mesh=mesh, in_specs=in_specs, out_specs=out_specs, check_vma=False
    )
```

profile of v0, /device:TPU:0, one launch (start us, length us, event | category | flops | bytes accessed | tf_op | source)
XLA Modules:
  0.0 341.7 jit_solution(962298888700188795)
XLA Ops:
  2.3 6.0 %collective-permute-start.1 = (f32[1,48,816]{2,1,0:T(8,128)S(1)}, f32[1,48,816]{2,1,0:T(8,128)S(1)}, u32[]{:S(2)}, u32[]{:S(2)}) collective-permute-start(f32[1,48,816]{2,1,0:T(8,128)S(1)} %get-tuple-element.30), channel_id=1, source_target_pairs={{4,0},{8,4},{12,8},{16,12},{20,16},{24,20},{28,24},{0,28},{5,1},{9... | collective-permute-start | bytes 470024 | tf_op jit(solution)/shard_map/ppermute | solution.py:17
  9.9 40.1 %all-reduce.2 = s32[32]{0:T(128)S(1)} all-reduce(s32[32]{0:T(128)S(1)} %dynamic-update-slice), channel_id=1, replica_groups=mesh['gx'=8,'gy'=4] {'gx','gy'}, use_global_device_ids=true, to_apply=%add.2 | all-reduce | flops 32 | bytes 256
  53.0 9.2 %scatter_custom_fusion = s32[1152]{0:T(1024)S(1)} fusion(s32[1152]{0:T(1024)S(1)} %fusion.21, s32[1152]{0:T(1024)S(1)} %broadcast.571, s32[]{:T(128)} %constant.140.clone.1), kind=kCustom, calls=%fused_computation.112 | custom fusion | flops 1152 | bytes 4612 | tf_op jit(solution)/shard_map/scatter-add | solution.py:81
  63.7 6.5 %gather_fusion = s32[1152]{0:T(1024)S(1)} fusion(s32[1152]{0:T(1024)S(1)} %fusion.17, s32[2048]{0:T(1024)S(1)} %pad_clamp_fusion.3), kind=kCustom, calls=%fused_computation | custom fusion | bytes 13824 | tf_op jit(solution)/shard_map/gather | solution.py:87
  70.3 1.6 pad_maximum_fusion.19
  73.2 5.7 %broadcast_in_dim.87 = f32[25,48,12,66]{3,2,1,0:T(8,128)} broadcast(f32[25,48,12]{2,1,0:T(8,128)S(1)} %broadcast_minimum_fusion), dimensions={0,1,2} | broadcast | bytes 3859200 | tf_op jit(solution)/shard_map/broadcast_in_dim | solution.py:49
  78.9 9.2 %min.15 = f32[25,48,792]{2,1,0:T(8,128)} reshape(f32[25,48,12,66]{3,2,1,0:T(8,128)} %broadcast_in_dim.87) | data formatting | bytes 7603200 | tf_op jit(solution)/shard_map/min | solution.py:50
  88.1 5.7 %broadcast_in_dim.86 = f32[25,48,12,66]{3,2,1,0:T(8,128)} broadcast(f32[25,48,12]{2,1,0:T(8,128)S(1)} %get-tuple-element.23), dimensions={0,1,2} | broadcast | bytes 3859200 | tf_op jit(solution)/shard_map/broadcast_in_dim | solution.py:49
  93.8 9.2 %max.26 = f32[25,48,792]{2,1,0:T(8,128)} reshape(f32[25,48,12,66]{3,2,1,0:T(8,128)} %broadcast_in_dim.86) | data formatting | bytes 7603200 | tf_op jit(solution)/shard_map/max | solution.py:50
  103.0 8.9 %fusion.4 = f32[25,48,792]{2,1,0:T(8,128)} fusion(f32[25,48,792]{2,1,0:T(8,128)} %min.15, f32[1,48,816]{2,1,0:T(8,128)S(1)} %collective-permute-done.1, f32[24,48,24]{2,1,0:T(8,128)S(1)} %copy.91, f32[24,48,792]{2,1,0:T(8,128)} %param.5, f32[25,48,792]{2,1,0:T(8,128)} %max.26, f32[1,48,816]{2,1,0:T(8,128)S(1)} %collective-permute-done), kind=kLoop, calls=%fused_computation.21 | loop fusion | flops 6652800 | bytes 15478272 | tf_op jit(solution)/shard_map/add | solution.py:50
  113.7 5.6 %broadcast_in_dim.89 = f32[24,49,12,66]{3,2,0,1:T(8,128)} broadcast(f32[24,49,12]{2,0,1:T(8,128)S(1)} %copy.96), dimensions={0,1,2} | broadcast | bytes 3782016 | tf_op jit(solution)/shard_map/broadcast_in_dim | solution.py:52
  119.3 9.1 %min.17 = f32[24,49,792]{2,0,1:T(8,128)} reshape(f32[24,49,12,66]{3,2,0,1:T(8,128)} %broadcast_in_dim.89) | data formatting | bytes 7451136 | tf_op jit(solution)/shard_map/min | solution.py:53
  128.7 5.6 %broadcast_in_dim.88 = f32[24,49,12,66]{3,2,0,1:T(8,128)} broadcast(f32[24,49,12]{2,0,1:T(8,128)S(1)} %copy.94), dimensions={0,1,2} | broadcast | bytes 3782016 | tf_op jit(solution)/shard_map/broadcast_in_dim | solution.py:52
  134.3 9.1 %max.28 = f32[24,49,792]{2,0,1:T(8,128)} reshape(f32[24,49,12,66]{3,2,0,1:T(8,128)} %broadcast_in_dim.88) | data formatting | bytes 7451136 | tf_op jit(solution)/shard_map/max | solution.py:53
  143.4 8.6 %fusion.1 = f32[24,49,792]{2,1,0:T(8,128)S(1)} fusion(f32[26,1,816]{2,1,0:T(1,128)S(1)} %collective-permute-done.3, f32[1,48,816]{2,1,0:T(8,128)S(1)} %collective-permute-done.1, f32[1,48,816]{2,1,0:T(8,128)S(1)} %collective-permute-done, f32[24,48,24]{2,1,0:T(8,128)S(1)} %copy.91, f32[24,48,792]{2,1,0:T(8,128)} %param.5, ...), kind=kLoop, calls=%fused_computation.10 | loop fusion | flops 10245312 | bytes 15419904 | tf_op jit(solution)/shard_map/add | solution.py:53
  152.0 5.4 %fusion.36 = (bf16[24,48,792]{2,1,0:T(8,128)(2,1)S(1)}, f32[24,48,792]{2,1,0:T(8,128)}) fusion(f32[24,49,792]{2,1,0:T(8,128)S(1)} %fusion.1, f32[24,48,792]{2,1,0:T(8,128)S(1)} %copy-done.2, f32[25,48,792]{2,1,0:T(8,128)} %fusion.4), kind=kLoop, calls=%fused_computation.134 | loop fusion | flops 4561920 | bytes 23721984 | tf_op jit(solution)/shard_map/convert_element_type | solution.py:69
  157.4 4.9 %gather_fusion.1 = bf16[1152,792]{1,0:T(8,128)(2,1)} fusion(bf16[1152,792]{1,0:T(8,128)(2,1)S(1)} %bitcast.67, s32[2048]{0:T(1024)S(1)} %pad_clamp_fusion.2), kind=kCustom, calls=%fused_computation.1 | custom fusion | bytes 3654144 | tf_op jit(solution)/shard_map/gather | solution.py:87
  162.3 3.9 %copy_select_fusion = bf16[36,32,792]{2,0,1:T(8,128)(2,1)} fusion(bf16[36,32,792]{2,1,0:T(8,128)(2,1)} %bitcast.70, pred[36,32]{0,1:T(8,128)(4,1)S(1)} %copy.99), kind=kLoop, calls=%fused_computation.32 | loop fusion | flops 912384 | bytes 3650688 | tf_op jit(solution)/shard_map/jit(_where)/select_n | solution.py:86
  166.2 5.9 %all-to-all-start = ((bf16[36,32,792]{2,0,1:T(8,128)(2,1)}), bf16[36,32,792]{2,0,1:T(8,128)(2,1)S(1)}, u32[]{:S(2)}, u32[]{:S(2)}) async-start(bf16[36,32,792]{2,0,1:T(8,128)(2,1)} %copy_select_fusion), calls=%async_computation | async-start | bytes 4587520 | tf_op jit(solution)/shard_map/all_to_all | solution.py:98
  175.6 49.4 %all-to-all-done = bf16[36,32,792]{2,0,1:T(8,128)(2,1)S(1)} async-done(((bf16[36,32,792]{2,0,1:T(8,128)(2,1)}), bf16[36,32,792]{2,0,1:T(8,128)(2,1)S(1)}, u32[]{:S(2)}, u32[]{:S(2)}) %all-to-all-start) | async-done | bytes 1824800 | tf_op jit(solution)/shard_map/all_to_all | solution.py:98
  224.9 1.6 copy.101
  226.5 2.9 gather_fusion.3
  230.2 6.1 %multiply_convert_fusion = bf16[1728,66,66]{0,2,1:T(8,128)(2,1)} fusion(f32[1728,66]{0,1:T(8,128)S(1)} %copy.102), kind=kLoop, calls=%fused_computation.7 | loop fusion | flops 15054336 | bytes 15510528 | tf_op jit(solution)/shard_map/while/body/eval_jaxpr/convert_element_type | solution.py:31
  236.3 20.8 %convert_element_type.60 = bf16[1728,4356]{0,1:T(8,128)(2,1)} reshape(bf16[1728,66,66]{0,2,1:T(8,128)(2,1)} %multiply_convert_fusion) | data formatting | bytes 30108672 | tf_op jit(solution)/shard_map/while/body/eval_jaxpr/convert_element_type | solution.py:31
  257.1 7.7 %fusion.9 = bf16[1728,128]{0,1:T(8,128)(2,1)S(1)} fusion(bf16[1728,4356]{0,1:T(8,128)(2,1)} %convert_element_type.60, bf16[4356,66]{0,1:T(8,128)(2,1)S(1)} %copy-done.4), kind=kOutput, calls=%fused_computation.33 | convolution fusion | flops 1926955008 | bytes 16071696 | tf_op jit(solution)/shard_map/while/body/eval_jaxpr/dot_general | solution.py:32
  265.5 4.7 %gather_fusion.4 = bf16[1152,792]{1,0:T(8,128)(2,1)S(1)} fusion(bf16[145,792]{1,0:T(8,128)(2,1)S(1)} %concatenate.36, s32[2048]{0:T(1024)S(1)} %pad_clamp_fusion.1), kind=kCustom, calls=%fused_computation.4 | custom fusion | bytes 3654144 | tf_op jit(solution)/shard_map/gather | solution.py:103
  270.2 2.0 copy.105
  272.3 4.3 %all-to-all-start.1 = ((bf16[36,32,792]{2,0,1:T(8,128)(2,1)}), bf16[36,32,792]{2,0,1:T(8,128)(2,1)}, u32[]{:S(2)}, u32[]{:S(2)}) async-start(bf16[36,32,792]{2,0,1:T(8,128)(2,1)} %copy.105), calls=%async_computation.1 | async-start | bytes 4587520 | tf_op jit(solution)/shard_map/all_to_all | solution.py:102
  278.0 51.6 %all-to-all-done.1 = bf16[36,32,792]{2,0,1:T(8,128)(2,1)} async-done(((bf16[36,32,792]{2,0,1:T(8,128)(2,1)}), bf16[36,32,792]{2,0,1:T(8,128)(2,1)}, u32[]{:S(2)}, u32[]{:S(2)}) %all-to-all-start.1) | async-done | bytes 1824800 | tf_op jit(solution)/shard_map/all_to_all | solution.py:102
  329.6 1.9 copy.106
  331.5 4.9 %gather_fusion.5 = bf16[1152,792]{1,0:T(8,128)(2,1)} fusion(bf16[1152,792]{1,0:T(8,128)(2,1)S(1)} %bitcast.68, s32[2048]{0:T(1024)S(1)} %pad_clamp_fusion), kind=kCustom, calls=%fused_computation.5 | custom fusion | bytes 3654144 | tf_op jit(solution)/shard_map/gather | solution.py:112
  336.4 5.3 %fusion.8 = f32[24,48,792]{2,1,0:T(8,128)} fusion(f32[24,48,792]{2,1,0:T(8,128)} %get-tuple-element.22, bf16[24,48,792]{2,1,0:T(8,128)(2,1)} %bitcast.72, pred[24,48]{1,0:T(8,128)(4,1)S(1)} %broadcast_compare_fusion.1), kind=kLoop, calls=%fused_computation.31 | loop fusion | flops 2737152 | bytes 9124992 | tf_op jit(solution)/shard_map/add | solution.py:113
  (93 shorter events, 17.9 us)
Async XLA Ops:
  0.0 8.3 %copy-start.5 = (s32[24,48]{1,0:T(8,128)S(1)}, s32[24,48]{1,0:T(8,128)}, u32[]{:S(2)}) copy-start(s32[24,48]{1,0:T(8,128)} %param.7) | copy-start | bytes 13828
  2.3 68.0 %collective-permute-start.1 = (f32[1,48,816]{2,1,0:T(8,128)S(1)}, f32[1,48,816]{2,1,0:T(8,128)S(1)}, u32[]{:S(2)}, u32[]{:S(2)}) collective-permute-start(f32[1,48,816]{2,1,0:T(8,128)S(1)} %get-tuple-element.30), channel_id=1, source_target_pairs={{4,0},{8,4},{12,8},{16,12},{20,16},{24,20},{28,24},{0,28},{5,1},{9... | collective-permute-start | bytes 470024 | tf_op jit(solution)/shard_map/ppermute | solution.py:17
  8.3 61.9 %collective-permute-start = (f32[1,48,816]{2,1,0:T(8,128)S(1)}, f32[1,48,816]{2,1,0:T(8,128)S(1)}, u32[]{:S(2)}, u32[]{:S(2)}) collective-permute-start(f32[1,48,816]{2,1,0:T(8,128)S(1)} %get-tuple-element.29), channel_id=1, source_target_pairs={{0,4},{4,8},{8,12},{12,16},{16,20},{20,24},{24,28},{28,0},{1,5},{5... | collective-permute-start | bytes 470024 | tf_op jit(solution)/shard_map/ppermute | solution.py:16
  70.2 2.6 copy-start
  71.9 40.0 %collective-permute-start.3 = (f32[26,1,816]{2,1,0:T(1,128)S(1)}, f32[26,1,816]{2,1,0:T(1,128)S(1)}, u32[]{:S(2)}, u32[]{:S(2)}) collective-permute-start(f32[26,1,816]{2,1,0:T(1,128)S(1)} %get-tuple-element.28), channel_id=1, source_target_pairs={{1,0},{2,1},{3,2},{0,3},{5,4},{6,5},{7,6},{4,7},{9,8},{10,9},{11,1... | collective-permute-start | bytes 254600 | tf_op jit(solution)/shard_map/ppermute | solution.py:17
  72.0 39.9 %collective-permute-start.2 = (f32[26,1,816]{2,1,0:T(1,128)S(1)}, f32[26,1,816]{2,1,0:T(1,128)S(1)}, u32[]{:S(2)}, u32[]{:S(2)}) collective-permute-start(f32[26,1,816]{2,1,0:T(1,128)S(1)} %get-tuple-element.27), channel_id=1, source_target_pairs={{0,1},{1,2},{2,3},{3,0},{4,5},{5,6},{6,7},{7,4},{8,9},{9,10},{10,1... | collective-permute-start | bytes 254600 | tf_op jit(solution)/shard_map/ppermute | solution.py:16
  103.0 8.9 %copy-start.1 = (f32[24,48,792]{2,1,0:T(8,128)S(1)}, f32[24,48,792]{2,1,0:T(8,128)}, u32[]{:S(2)}) copy-start(f32[24,48,792]{2,1,0:T(8,128)} %param.5) | copy-start | bytes 10948612
  143.4 8.6 %copy-start.2 = (f32[24,48,792]{2,1,0:T(8,128)S(1)}, f32[24,48,792]{2,1,0:T(8,128)}, u32[]{:S(2)}) copy-start(f32[24,48,792]{2,1,0:T(8,128)} %param.5) | copy-start | bytes 10948612
  162.3 11.5 %copy-start.6 = (s32[6,6]{1,0:T(8,128)S(1)}, s32[6,6]{1,0:T(8,128)}, u32[]{:S(2)}) copy-start(s32[6,6]{1,0:T(8,128)} %param.9) | copy-start | bytes 436
  162.3 12.3 %copy-start.3 = (bf16[4356,66]{0,1:T(8,128)(2,1)S(1)}, bf16[4356,66]{0,1:T(8,128)(2,1)}, u32[]{:S(2)}) copy-start(bf16[4356,66]{0,1:T(8,128)(2,1)} %param.8) | copy-start | bytes 1724980
  166.2 58.7 %all-to-all-start = ((bf16[36,32,792]{2,0,1:T(8,128)(2,1)}), bf16[36,32,792]{2,0,1:T(8,128)(2,1)S(1)}, u32[]{:S(2)}, u32[]{:S(2)}) async-start(bf16[36,32,792]{2,0,1:T(8,128)(2,1)} %copy_select_fusion), calls=%async_computation | async-start | bytes 4587520 | tf_op jit(solution)/shard_map/all_to_all | solution.py:98
  236.3 20.8 %copy-start.4 = (bf16[4356,66]{0,1:T(8,128)(2,1)S(1)}, bf16[4356,66]{0,1:T(8,128)(2,1)}, u32[]{:S(2)}) copy-start(bf16[4356,66]{0,1:T(8,128)(2,1)} %broadcast_select_fusion) | copy-start | bytes 1724980
  272.3 57.3 %all-to-all-start.1 = ((bf16[36,32,792]{2,0,1:T(8,128)(2,1)}), bf16[36,32,792]{2,0,1:T(8,128)(2,1)}, u32[]{:S(2)}, u32[]{:S(2)}) async-start(bf16[36,32,792]{2,0,1:T(8,128)(2,1)} %copy.105), calls=%async_computation.1 | async-start | bytes 4587520 | tf_op jit(solution)/shard_map/all_to_all | solution.py:102
where the time goes:
time: 343 us; the launch traced here: 342 us
  local copies, waits for them, and re-layouts  118 us (34%)
  waiting for transfers between devices  101 us (29%)
  other arithmetic  57.7 us (17%)
  blocking collectives  40.1 us (12%)
  starting transfers between devices  16.7 us (5%)
  matrix products  8.16 us (2%)
    all_to_all x1, waiting for transfers between devices, per_device(): lax.all_to_all(extended[slot_of.reshape(-1)].reshape(send_rows, devices,...  51.6 us
    all_to_all x1, waiting for transfers between devices, per_device(): lax.all_to_all(outgoing, ('gx', 'gy'), split_axis=1, concat_axis=1, tiled...  49.4 us
    unnamed x1, blocking collectives  40.1 us
    convert_element_type x1, local copies, waits for them, and re-layouts, one_block(): (wide[:, :, None] * wide[:, None, :]).astype(jnp.bfloat16)  20.8 us
    broadcast_in_dim x2, local copies, waits for them, and re-layouts, per_device(): jnp.repeat(0.5 * (wind_x[:-1, 1:-1] + wind_x[1:, 1:-1]), chan, axis=2)  11.3 us
    broadcast_in_dim x2, local copies, waits for them, and re-layouts, per_device(): jnp.repeat(0.5 * (wind_y[1:-1, :-1] + wind_y[1:-1, 1:]), chan, axis=2)  11.2 us
    max x2, local copies, waits for them, and re-layouts, per_device(): jnp.maximum(face_y, 0.0) * along_y[:, :-1]  9.41 us
    min x2, local copies, waits for them, and re-layouts, per_device(): jnp.minimum(face_y, 0.0) * along_y[:, 1:]  9.41 us
  transfers between devices with their start and end apart: 6, of which 2 were waited for; matrix products, arithmetic and copies ran while one was open for 19% of the time, Pallas kernels for 0%

commit v1 on v0

--- a/solution.py
+++ b/solution.py
@@ -95,7 +95,12 @@
     source_dev = jnp.sum((ends[None, :] <= global_rank[:, None]).astype(jnp.int32), axis=1)
     local_rank = global_rank - starts[source_dev]
     arrive_row = local_rank // devices * devices + source_dev
-    arrived = lax.all_to_all(outgoing, ("gx", "gy"), split_axis=1, concat_axis=1, tiled=True)
+    arrived = jnp.concatenate(
+        lax.all_to_all(
+            jnp.stack(jnp.split(outgoing, lax.axis_size(("gx", "gy")), axis=1)), ("gx", "gy"), 0, 0
+        ),
+        axis=1,
+    )
     gathered = arrived.reshape(send_rows * devices, width)[arrive_row]
     computed = coalesce(gathered, chan, kernel_wide)
     extended = jnp.concatenate([computed, jnp.zeros((1, width), jnp.bfloat16)], axis=0)

time: 343 us -> 362 us (1.055)
  local copies, waits for them, and re-layouts: 118 us -> 138 us
    unnamed x19 -> x50, local copies, waits for them, and re-layouts: 2.91 us -> 22.5 us
  transfers between devices with their start and end apart: 6 -> 6, of which waited for: 2 -> 2; matrix products, arithmetic and copies ran while one was open for 19% -> 18% of each run, Pallas kernels for 0% -> 0%
where the time goes in v1:
time: 362 us; the launch traced here: 361 us
  local copies, waits for them, and re-layouts  138 us (38%)
  waiting for transfers between devices  101 us (28%)
  other arithmetic  56.3 us (16%)
  blocking collectives  40.1 us (11%)
  starting transfers between devices  16.7 us (5%)
  matrix products  8.16 us (2%)
    all_to_all x1, waiting for transfers between devices, per_device(): lax.all_to_all(extended[slot_of.reshape(-1)].reshape(send_rows, devices,...  51.6 us
    all_to_all x1, waiting for transfers between devices, per_device(): lax.all_to_all(jnp.stack(jnp.split(outgoing, lax.axis_size(('gx', 'gy')),...  49.6 us
    unnamed x1, blocking collectives  40.1 us
    unnamed x50, local copies, waits for them, and re-layouts  22.5 us
    convert_element_type x1, local copies, waits for them, and re-layouts, one_block(): (wide[:, :, None] * wide[:, None, :]).astype(jnp.bfloat16)  20.8 us
    broadcast_in_dim x2, local copies, waits for them, and re-layouts, per_device(): jnp.repeat(0.5 * (wind_x[:-1, 1:-1] + wind_x[1:, 1:-1]), chan, axis=2)  11.3 us
    broadcast_in_dim x2, local copies, waits for them, and re-layouts, per_device(): jnp.repeat(0.5 * (wind_y[1:-1, :-1] + wind_y[1:-1, 1:]), chan, axis=2)  11.2 us
    max x2, local copies, waits for them, and re-layouts, per_device(): jnp.maximum(face_y, 0.0) * along_y[:, :-1]  9.41 us
  transfers between devices with their start and end apart: 6, of which 2 were waited for; matrix products, arithmetic and copies ran while one was open for 18% of the time, Pallas kernels for 0%

profile of v1, /device:TPU:0, one launch (start us, length us, event | category | flops | bytes accessed | tf_op | source)
XLA Modules:
  0.0 360.8 jit_solution(12253043980687756776)
XLA Ops:
  2.3 6.0 %collective-permute-start.1 = (f32[1,48,816]{2,1,0:T(8,128)S(1)}, f32[1,48,816]{2,1,0:T(8,128)S(1)}, u32[]{:S(2)}, u32[]{:S(2)}) collective-permute-start(f32[1,48,816]{2,1,0:T(8,128)S(1)} %get-tuple-element.30), channel_id=1, source_target_pairs={{4,0},{8,4},{12,8},{16,12},{20,16},{24,20},{28,24},{0,28},{5,1},{9... | collective-permute-start | bytes 470024 | tf_op jit(solution)/shard_map/ppermute | solution.py:17
  9.8 40.1 %all-reduce.2 = s32[32]{0:T(128)S(1)} all-reduce(s32[32]{0:T(128)S(1)} %dynamic-update-slice), channel_id=1, replica_groups=mesh['gx'=8,'gy'=4] {'gx','gy'}, use_global_device_ids=true, to_apply=%add.2 | all-reduce | flops 32 | bytes 256
  53.2 9.2 %scatter_custom_fusion = s32[1152]{0:T(1024)S(1)} fusion(s32[1152]{0:T(1024)S(1)} %fusion.53, s32[1152]{0:T(1024)S(1)} %broadcast.571, s32[]{:T(128)} %constant.140.clone.1), kind=kCustom, calls=%fused_computation.176 | custom fusion | flops 1152 | bytes 4612 | tf_op jit(solution)/shard_map/scatter-add | solution.py:81
  64.0 6.5 %gather_fusion = s32[1152]{0:T(1024)S(1)} fusion(s32[1152]{0:T(1024)S(1)} %fusion.49, s32[2048]{0:T(1024)S(1)} %pad_clamp_fusion.3), kind=kCustom, calls=%fused_computation | custom fusion | bytes 13824 | tf_op jit(solution)/shard_map/gather | solution.py:87
  70.5 1.6 pad_maximum_fusion.19
  73.5 5.7 %broadcast_in_dim.87 = f32[25,48,12,66]{3,2,1,0:T(8,128)} broadcast(f32[25,48,12]{2,1,0:T(8,128)S(1)} %broadcast_minimum_fusion), dimensions={0,1,2} | broadcast | bytes 3859200 | tf_op jit(solution)/shard_map/broadcast_in_dim | solution.py:49
  79.2 9.2 %min.15 = f32[25,48,792]{2,1,0:T(8,128)} reshape(f32[25,48,12,66]{3,2,1,0:T(8,128)} %broadcast_in_dim.87) | data formatting | bytes 7603200 | tf_op jit(solution)/shard_map/min | solution.py:50
  88.4 5.7 %broadcast_in_dim.86 = f32[25,48,12,66]{3,2,1,0:T(8,128)} broadcast(f32[25,48,12]{2,1,0:T(8,128)S(1)} %get-tuple-element.23), dimensions={0,1,2} | broadcast | bytes 3859200 | tf_op jit(solution)/shard_map/broadcast_in_dim | solution.py:49
  94.0 9.2 %max.26 = f32[25,48,792]{2,1,0:T(8,128)} reshape(f32[25,48,12,66]{3,2,1,0:T(8,128)} %broadcast_in_dim.86) | data formatting | bytes 7603200 | tf_op jit(solution)/shard_map/max | solution.py:50
  103.3 8.9 %fusion.4 = f32[25,48,792]{2,1,0:T(8,128)} fusion(f32[25,48,792]{2,1,0:T(8,128)} %min.15, f32[1,48,816]{2,1,0:T(8,128)S(1)} %collective-permute-done.1, f32[24,48,24]{2,1,0:T(8,128)S(1)} %copy.126, f32[24,48,792]{2,1,0:T(8,128)} %param.5, f32[25,48,792]{2,1,0:T(8,128)} %max.26, f32[1,48,816]{2,1,0:T(8,128)S(1)} %collective-permute-done), kind=kLoop, calls=%fused_computation.21 | loop fusion | flops 6652800 | bytes 15478272 | tf_op jit(solution)/shard_map/add | solution.py:50
  114.0 5.6 %broadcast_in_dim.89 = f32[24,49,12,66]{3,2,0,1:T(8,128)} broadcast(f32[24,49,12]{2,0,1:T(8,128)S(1)} %copy.131), dimensions={0,1,2} | broadcast | bytes 3782016 | tf_op jit(solution)/shard_map/broadcast_in_dim | solution.py:52
  119.6 9.1 %min.17 = f32[24,49,792]{2,0,1:T(8,128)} reshape(f32[24,49,12,66]{3,2,0,1:T(8,128)} %broadcast_in_dim.89) | data formatting | bytes 7451136 | tf_op jit(solution)/shard_map/min | solution.py:53
  129.0 5.6 %broadcast_in_dim.88 = f32[24,49,12,66]{3,2,0,1:T(8,128)} broadcast(f32[24,49,12]{2,0,1:T(8,128)S(1)} %copy.129), dimensions={0,1,2} | broadcast | bytes 3782016 | tf_op jit(solution)/shard_map/broadcast_in_dim | solution.py:52
  134.6 9.1 %max.28 = f32[24,49,792]{2,0,1:T(8,128)} reshape(f32[24,49,12,66]{3,2,0,1:T(8,128)} %broadcast_in_dim.88) | data formatting | bytes 7451136 | tf_op jit(solution)/shard_map/max | solution.py:53
  143.7 8.6 %fusion.1 = f32[24,49,792]{2,1,0:T(8,128)S(1)} fusion(f32[26,1,816]{2,1,0:T(1,128)S(1)} %collective-permute-done.3, f32[1,48,816]{2,1,0:T(8,128)S(1)} %collective-permute-done.1, f32[1,48,816]{2,1,0:T(8,128)S(1)} %collective-permute-done, f32[24,48,24]{2,1,0:T(8,128)S(1)} %copy.126, f32[24,48,792]{2,1,0:T(8,128)} %param.5, ...), kind=kLoop, calls=%fused_computation.10 | loop fusion | flops 10245312 | bytes 15419904 | tf_op jit(solution)/shard_map/add | solution.py:53
  152.3 5.4 %fusion.68 = (bf16[24,48,792]{2,1,0:T(8,128)(2,1)S(1)}, f32[24,48,792]{2,1,0:T(8,128)}) fusion(f32[24,49,792]{2,1,0:T(8,128)S(1)} %fusion.1, f32[24,48,792]{2,1,0:T(8,128)S(1)} %copy-done.2, f32[25,48,792]{2,1,0:T(8,128)} %fusion.4), kind=kLoop, calls=%fused_computation.198 | loop fusion | flops 4561920 | bytes 23721984 | tf_op jit(solution)/shard_map/convert_element_type | solution.py:69
  157.8 4.9 %gather_fusion.1 = bf16[1152,792]{1,0:T(8,128)(2,1)} fusion(bf16[1152,792]{1,0:T(8,128)(2,1)S(1)} %bitcast.196, s32[2048]{0:T(1024)S(1)} %get-tuple-element.40), kind=kCustom, calls=%fused_computation.1 | custom fusion | bytes 3654144 | tf_op jit(solution)/shard_map/gather | solution.py:87
  162.7 2.5 copy_select_fusion
  185.4 5.8 %all-to-all-start = ((bf16[32,36,1,792]{3,1,2,0:T(8,128)(2,1)}), bf16[32,36,1,792]{3,1,2,0:T(8,128)(2,1)S(1)}, u32[]{:S(2)}, u32[]{:S(2)}) async-start(bf16[32,36,1,792]{3,1,2,0:T(8,128)(2,1)} %fusion.14), calls=%async_computation | async-start | bytes 4587520 | tf_op jit(solution)/shard_map/all_to_all | solution.py:99
  194.4 49.6 %all-to-all-done = bf16[32,36,1,792]{3,1,2,0:T(8,128)(2,1)S(1)} async-done(((bf16[32,36,1,792]{3,1,2,0:T(8,128)(2,1)}), bf16[32,36,1,792]{3,1,2,0:T(8,128)(2,1)S(1)}, u32[]{:S(2)}, u32[]{:S(2)}) %all-to-all-start) | async-done | bytes 1824800 | tf_op jit(solution)/shard_map/all_to_all | solution.py:99
  244.0 1.6 copy.136
  245.6 2.9 gather_fusion.3
  249.3 6.1 %multiply_convert_fusion = bf16[1728,66,66]{0,2,1:T(8,128)(2,1)} fusion(f32[1728,66]{0,1:T(8,128)S(1)} %copy.137), kind=kLoop, calls=%fused_computation.7 | loop fusion | flops 15054336 | bytes 15510528 | tf_op jit(solution)/shard_map/while/body/eval_jaxpr/convert_element_type | solution.py:31
  255.4 20.8 %convert_element_type.60 = bf16[1728,4356]{0,1:T(8,128)(2,1)} reshape(bf16[1728,66,66]{0,2,1:T(8,128)(2,1)} %multiply_convert_fusion) | data formatting | bytes 30108672 | tf_op jit(solution)/shard_map/while/body/eval_jaxpr/convert_element_type | solution.py:31
  276.2 7.7 %fusion.9 = bf16[1728,128]{0,1:T(8,128)(2,1)S(1)} fusion(bf16[1728,4356]{0,1:T(8,128)(2,1)} %convert_element_type.60, bf16[4356,66]{0,1:T(8,128)(2,1)S(1)} %copy-done.4), kind=kOutput, calls=%fused_computation.33 | convolution fusion | flops 1926955008 | bytes 16071696 | tf_op jit(solution)/shard_map/while/body/eval_jaxpr/dot_general | solution.py:32
  284.6 4.7 %gather_fusion.4 = bf16[1152,792]{1,0:T(8,128)(2,1)S(1)} fusion(bf16[145,792]{1,0:T(8,128)(2,1)S(1)} %concatenate.36, s32[2048]{0:T(1024)S(1)} %get-tuple-element.39), kind=kCustom, calls=%fused_computation.4 | custom fusion | bytes 3654144 | tf_op jit(solution)/shard_map/gather | solution.py:108
  289.3 2.0 copy.140
  291.4 4.3 %all-to-all-start.1 = ((bf16[36,32,792]{2,0,1:T(8,128)(2,1)}), bf16[36,32,792]{2,0,1:T(8,128)(2,1)}, u32[]{:S(2)}, u32[]{:S(2)}) async-start(bf16[36,32,792]{2,0,1:T(8,128)(2,1)} %copy.140), calls=%async_computation.1 | async-start | bytes 4587520 | tf_op jit(solution)/shard_map/all_to_all | solution.py:107
  297.1 51.6 %all-to-all-done.1 = bf16[36,32,792]{2,0,1:T(8,128)(2,1)} async-done(((bf16[36,32,792]{2,0,1:T(8,128)(2,1)}), bf16[36,32,792]{2,0,1:T(8,128)(2,1)}, u32[]{:S(2)}, u32[]{:S(2)}) %all-to-all-start.1) | async-done | bytes 1824800 | tf_op jit(solution)/shard_map/all_to_all | solution.py:107
  348.7 1.9 copy.141
  350.6 4.9 %gather_fusion.5 = bf16[1152,792]{1,0:T(8,128)(2,1)} fusion(bf16[1152,792]{1,0:T(8,128)(2,1)S(1)} %bitcast.197, s32[2048]{0:T(1024)S(1)} %pad_clamp_fusion), kind=kCustom, calls=%fused_computation.5 | custom fusion | bytes 3654144 | tf_op jit(solution)/shard_map/gather | solution.py:117
  355.5 5.3 %fusion.8 = f32[24,48,792]{2,1,0:T(8,128)} fusion(f32[24,48,792]{2,1,0:T(8,128)} %get-tuple-element.22, bf16[24,48,792]{2,1,0:T(8,128)(2,1)} %bitcast.202, pred[24,48]{1,0:T(8,128)(4,1)S(1)} %broadcast_compare_fusion.1), kind=kLoop, calls=%fused_computation.31 | loop fusion | flops 2737152 | bytes 9124992 | tf_op jit(solution)/shard_map/add | solution.py:118
  (124 shorter events, 38.2 us)
Async XLA Ops:
  1.2 7.1 %copy-start.5 = (s32[24,48]{1,0:T(8,128)S(1)}, s32[24,48]{1,0:T(8,128)}, u32[]{:S(2)}) copy-start(s32[24,48]{1,0:T(8,128)} %param.7) | copy-start | bytes 13828
  2.3 68.2 %collective-permute-start.1 = (f32[1,48,816]{2,1,0:T(8,128)S(1)}, f32[1,48,816]{2,1,0:T(8,128)S(1)}, u32[]{:S(2)}, u32[]{:S(2)}) collective-permute-start(f32[1,48,816]{2,1,0:T(8,128)S(1)} %get-tuple-element.30), channel_id=1, source_target_pairs={{4,0},{8,4},{12,8},{16,12},{20,16},{24,20},{28,24},{0,28},{5,1},{9... | collective-permute-start | bytes 470024 | tf_op jit(solution)/shard_map/ppermute | solution.py:17
  8.3 62.2 %collective-permute-start = (f32[1,48,816]{2,1,0:T(8,128)S(1)}, f32[1,48,816]{2,1,0:T(8,128)S(1)}, u32[]{:S(2)}, u32[]{:S(2)}) collective-permute-start(f32[1,48,816]{2,1,0:T(8,128)S(1)} %get-tuple-element.29), channel_id=1, source_target_pairs={{0,4},{4,8},{8,12},{12,16},{16,20},{20,24},{24,28},{28,0},{1,5},{5... | collective-permute-start | bytes 470024 | tf_op jit(solution)/shard_map/ppermute | solution.py:16
  70.5 2.6 copy-start
  72.2 40.0 %collective-permute-start.3 = (f32[26,1,816]{2,1,0:T(1,128)S(1)}, f32[26,1,816]{2,1,0:T(1,128)S(1)}, u32[]{:S(2)}, u32[]{:S(2)}) collective-permute-start(f32[26,1,816]{2,1,0:T(1,128)S(1)} %get-tuple-element.28), channel_id=1, source_target_pairs={{1,0},{2,1},{3,2},{0,3},{5,4},{6,5},{7,6},{4,7},{9,8},{10,9},{11,1... | collective-permute-start | bytes 254600 | tf_op jit(solution)/shard_map/ppermute | solution.py:17
  72.2 39.9 %collective-permute-start.2 = (f32[26,1,816]{2,1,0:T(1,128)S(1)}, f32[26,1,816]{2,1,0:T(1,128)S(1)}, u32[]{:S(2)}, u32[]{:S(2)}) collective-permute-start(f32[26,1,816]{2,1,0:T(1,128)S(1)} %get-tuple-element.27), channel_id=1, source_target_pairs={{0,1},{1,2},{2,3},{3,0},{4,5},{5,6},{6,7},{7,4},{8,9},{9,10},{10,1... | collective-permute-start | bytes 254600 | tf_op jit(solution)/shard_map/ppermute | solution.py:16
  103.3 8.9 %copy-start.1 = (f32[24,48,792]{2,1,0:T(8,128)S(1)}, f32[24,48,792]{2,1,0:T(8,128)}, u32[]{:S(2)}) copy-start(f32[24,48,792]{2,1,0:T(8,128)} %param.5) | copy-start | bytes 10948612
  143.7 8.7 %copy-start.2 = (f32[24,48,792]{2,1,0:T(8,128)S(1)}, f32[24,48,792]{2,1,0:T(8,128)}, u32[]{:S(2)}) copy-start(f32[24,48,792]{2,1,0:T(8,128)} %param.5) | copy-start | bytes 10948612
  185.3 7.5 %copy-start.6 = (s32[6,6]{1,0:T(8,128)S(1)}, s32[6,6]{1,0:T(8,128)}, u32[]{:S(2)}) copy-start(s32[6,6]{1,0:T(8,128)} %param.9) | copy-start | bytes 436
  185.3 8.1 %copy-start.3 = (bf16[4356,66]{0,1:T(8,128)(2,1)S(1)}, bf16[4356,66]{0,1:T(8,128)(2,1)}, u32[]{:S(2)}) copy-start(bf16[4356,66]{0,1:T(8,128)(2,1)} %param.8) | copy-start | bytes 1724980
  185.4 58.7 %all-to-all-start = ((bf16[32,36,1,792]{3,1,2,0:T(8,128)(2,1)}), bf16[32,36,1,792]{3,1,2,0:T(8,128)(2,1)S(1)}, u32[]{:S(2)}, u32[]{:S(2)}) async-start(bf16[32,36,1,792]{3,1,2,0:T(8,128)(2,1)} %fusion.14), calls=%async_computation | async-start | bytes 4587520 | tf_op jit(solution)/shard_map/all_to_all | solution.py:99
  255.4 20.8 %copy-start.4 = (bf16[4356,66]{0,1:T(8,128)(2,1)S(1)}, bf16[4356,66]{0,1:T(8,128)(2,1)}, u32[]{:S(2)}) copy-start(bf16[4356,66]{0,1:T(8,128)(2,1)} %broadcast_select_fusion) | copy-start | bytes 1724980
  291.4 57.3 %all-to-all-start.1 = ((bf16[36,32,792]{2,0,1:T(8,128)(2,1)}), bf16[36,32,792]{2,0,1:T(8,128)(2,1)}, u32[]{:S(2)}, u32[]{:S(2)}) async-start(bf16[36,32,792]{2,0,1:T(8,128)(2,1)} %copy.140), calls=%async_computation.1 | async-start | bytes 4587520 | tf_op jit(solution)/shard_map/all_to_all | solution.py:107
